TPU v7x, 32 devices: a whole 2x2x4 slice. The times are simulated.
32 devices in a mesh: grp: 2 (over y), brick: 4 (over z), ray: 2 (over x), rep: 2 (over core).
Axes of the slice: x: 2, y: 2, z: 4, core: 2. Of those that a mesh axis runs over, the one named last changes fastest.
Arguments:
- samples: bfloat16 [32, 4, 16, 64], P(('grp', 'brick', 'ray', 'rep')), parts along dimension 0, may hold values from -6 to 6
- frequencies: float32 [16, 64], replicated, may hold values from -4 to 4
- w_first: bfloat16 [16, 128, 128], P('brick'), may hold values from -0.5 to 0.5
- w_second: bfloat16 [16, 128, 128], P('brick'), may hold values from -0.5 to 0.5
- w_out: bfloat16 [16, 4, 128], P('brick'), may hold values from -0.5 to 0.5
- brick_ids: int32 [32, 4], P(('grp', 'brick', 'ray', 'rep')), parts along dimension 0, may hold values from 0 to 15, as said below
- targets: float32 [3, 32], P(None, ('grp', 'brick', 'ray', 'rep')), parts along dimension 1, may hold values from -6 to 6
Outputs:
- prediction: float32 [3, 32], P(None, ('grp', 'brick', 'ray', 'rep')), parts along dimension 1
- grad_first: float32 [32, 128, 128], P(('grp', 'brick'), ('ray', 'rep')), parts along dimension 0
- grad_second: float32 [32, 128, 128], P(('grp', 'brick'), ('ray', 'rep')), parts along dimension 0
- grad_out: float32 [32, 4, 128], P(('grp', 'brick'), None, ('ray', 'rep')), parts along dimension 0
There are 2 independent parts, one for each index of `grp`. A program takes and returns all parts, laid end to end along the dimension named above; an argument that names none is the same for every part. Nothing has to cross between parts.
Inputs may be any that keep to these rules, and one draw needn't show every extreme that they name: `brick_ids`: the owner of brick id is id // 4. Among the 4 blocks of each of the 1 rays of one device (an aligned block of rows), at most 2 name bricks of any one owner; 1 owners get exactly 2 blocks from every device.
All inputs are finite; a program needn't handle non-finite values.
Results may differ from a plain program's by a relative error of at most 0.0055.
Values may be sent and summed in bfloat16 or wider, within the bound.
A program may use at most 64 MiB of HBM per device.

v0:
```python
import jax
import jax.numpy as jnp
from jax import lax
from jax.sharding import PartitionSpec as P

CAP = 2


loss_scale = 16.0


def silu_slope(values):
    squashed = jax.nn.sigmoid(values)
    return squashed * (1.0 + values * (1.0 - squashed))


def composite(field_rows):
    ray_rows = field_rows.shape[0]
    length = field_rows.shape[3]
    density = jax.nn.softplus(field_rows[:, :, 0, :]).reshape(ray_rows, -1)
    signal = jnp.moveaxis(field_rows[:, :, 1:, :], 2, 1).reshape(
        ray_rows, field_rows.shape[2] - 1, -1
    )
    optical = density * (1.0 / length)
    before = jnp.cumsum(optical, axis=1) - optical
    weights = jnp.exp(-before) * -jnp.expm1(-optical)
    return jnp.sum(weights[:, None, :] * signal, axis=2).T


def send_blocks(outgoing, labels):
    owners = lax.axis_size("brick")
    moved = (
        lax.all_to_all(
            outgoing.reshape((owners, CAP) + outgoing.shape[1:]),
            "brick",
            split_axis=0,
            concat_axis=0,
            tiled=True,
        ),
        lax.all_to_all(
            labels.reshape(owners, CAP), "brick", split_axis=0, concat_axis=0, tiled=True
        ),
    )
    return (moved[0].reshape(outgoing.shape), moved[1].reshape(labels.shape))


def trade_rows(rows_in):
    owners = lax.axis_size("brick")
    moved = lax.all_to_all(
        rows_in.reshape((owners, CAP) + rows_in.shape[1:]),
        "brick",
        split_axis=0,
        concat_axis=0,
        tiled=True,
    )
    return moved.reshape(rows_in.shape)


def per_brick(brick_table, slot_terms):
    summed = jnp.dot(
        brick_table.T, slot_terms.reshape(slot_terms.shape[0], -1), precision=lax.Precision.HIGHEST
    )
    return summed.reshape((brick_table.shape[1],) + slot_terms.shape[1:])


def on_device(samples, frequencies, w_first, w_second, w_out, brick_ids, targets):
    ray_rows, blocks_per_ray, channels, length = samples.shape
    bricks_here = w_first.shape[0]
    owners = lax.axis_size("brick")
    slot_total = owners * CAP
    block_count = ray_rows * blocks_per_ray
    flat_ids = brick_ids.reshape(block_count)
    owner_of = flat_ids // bricks_here
    local_id = flat_ids % bricks_here
    owner_table = (owner_of[:, None] == jnp.arange(owners, dtype=jnp.int32)[None, :]).astype(
        jnp.int32
    )
    earlier = jnp.cumsum(owner_table, axis=0) - owner_table
    incoming_rank = jnp.sum(earlier * owner_table, axis=1)
    slot_of = owner_of * CAP + incoming_rank
    outgoing = (
        jnp.zeros((slot_total, channels, length), jnp.bfloat16)
        .at[slot_of]
        .set(samples.reshape(block_count, channels, length))
    )
    labels = jnp.zeros((slot_total,), jnp.int32).at[slot_of].set(local_id)
    incoming, in_labels = send_blocks(outgoing, labels)
    phases = jnp.einsum(
        "scn,cf->snf", incoming.astype(jnp.float32), frequencies, precision=lax.Precision.HIGHEST
    )
    encoded_features = jnp.concatenate([jnp.sin(phases), jnp.cos(phases)], axis=-1).astype(
        jnp.bfloat16
    )
    first_layer = w_first[in_labels]
    second = w_second[in_labels]
    last = w_out[in_labels]
    first_preactivation = jnp.einsum(
        "kyd,kdc->kyc", encoded_features, first_layer, preferred_element_type=jnp.float32
    )
    hidden_first = jax.nn.silu(first_preactivation).astype(jnp.bfloat16)
    pre_second = jnp.einsum(
        "snh,shk->snk", hidden_first, second, preferred_element_type=jnp.float32
    )
    hidden_second = jax.nn.silu(pre_second).astype(jnp.bfloat16)
    field = jnp.einsum("snh,soh->son", hidden_second, last, preferred_element_type=jnp.float32)
    returned = trade_rows(field)
    own_fields = returned[slot_of].reshape(ray_rows, blocks_per_ray, field.shape[1], length)
    predicted, pullback = jax.vjp(composite, own_fields)
    (field_grad,) = pullback(loss_scale * (predicted - targets))
    grad_slots = (
        jnp.zeros((slot_total,) + field.shape[1:], jnp.float32)
        .at[slot_of]
        .set(field_grad.reshape((block_count,) + field.shape[1:]))
    )
    grad_rows = trade_rows(grad_slots).astype(jnp.bfloat16)
    slot_out = jnp.einsum(
        "son,snh->soh", grad_rows, hidden_second, preferred_element_type=jnp.float32
    )
    back_second = jnp.einsum("son,soh->snh", grad_rows, last, preferred_element_type=jnp.float32)
    d_second = (back_second * silu_slope(pre_second)).astype(jnp.bfloat16)
    slot_second = jnp.einsum(
        "snh,snk->shk", hidden_first, d_second, preferred_element_type=jnp.float32
    )
    back_first = jnp.einsum("snk,shk->snh", d_second, second, preferred_element_type=jnp.float32)
    first_layer_delta = (back_first * silu_slope(first_preactivation)).astype(jnp.bfloat16)
    first_layer_slot = jnp.einsum(
        "gmj,gmd->gjd", encoded_features, first_layer_delta, preferred_element_type=jnp.float32
    )
    brick_table = (in_labels[:, None] == jnp.arange(bricks_here, dtype=jnp.int32)[None, :]).astype(
        jnp.float32
    )
    grad_first = per_brick(brick_table, first_layer_slot)
    grad_second = per_brick(brick_table, slot_second)
    grad_last = per_brick(brick_table, slot_out)
    grad_first, grad_second, grad_last = lax.psum(
        (grad_first, grad_second, grad_last), ("ray", "rep")
    )
    group_index = lax.axis_index(("ray", "rep"))
    group_count = lax.axis_size(("ray", "rep"))
    wide_share = grad_first.shape[1] // group_count
    hidden_share = grad_second.shape[1] // group_count
    grad_first = lax.dynamic_slice_in_dim(grad_first, group_index * wide_share, wide_share, 1)
    grad_second = lax.dynamic_slice_in_dim(grad_second, group_index * hidden_share, hidden_share, 1)
    grad_last = lax.dynamic_slice_in_dim(grad_last, group_index * hidden_share, hidden_share, 2)
    return (predicted, grad_first, grad_second, grad_last)


def solution(mesh):
    return jax.shard_map(
        on_device,
        mesh=mesh,
        in_specs=(
            P(("grp", "brick", "ray", "rep"), None, None, None),
            P(),
            P("brick", None, None),
            P("brick", None, None),
            P("brick", None, None),
            P(("grp", "brick", "ray", "rep"), None),
            P(None, ("grp", "brick", "ray", "rep")),
        ),
        out_specs=(
            P(None, ("grp", "brick", "ray", "rep")),
            P(("grp", "brick"), ("ray", "rep"), None),
            P(("grp", "brick"), ("ray", "rep"), None),
            P(("grp", "brick"), None, ("ray", "rep")),
        ),
        check_vma=False,
    )
```

profile of v0, /device:TPU:0, one launch (start us, length us, event | category | flops | bytes accessed | tf_op | source)
XLA Modules:
  0.0 105.6 jit_solution(7217241128238730509)
XLA Ops:
  7.2 0.7 and_select_fusion
  8.0 0.2 select_reduce_fusion
  8.2 0.5 copy-done.6
  8.7 0.6 scatter_custom_fusion
  9.3 0.7 all_to_all.15
  9.9 6.3 %all-to-all-start = ((s32[4,1,2]{2,1,0:T(1,128)}), s32[4,1,2]{2,1,0:T(1,128)S(1)}, u32[]{:S(2)}, u32[]{:S(2)}) async-start(s32[4,1,2]{2,1,0:T(1,128)} %bitcast.4), calls=%async_computation | async-start | bytes 4096 | tf_op jit(solution)/shard_map/all_to_all | solution.py:40
  16.2 0.7 copy-done.2
  17.0 0.6 scatter_fusion
  17.6 0.7 reshape.759
  18.3 3.4 %all-to-all-done = s32[4,1,2]{2,1,0:T(1,128)S(1)} async-done(((s32[4,1,2]{2,1,0:T(1,128)}), s32[4,1,2]{2,1,0:T(1,128)S(1)}, u32[]{:S(2)}, u32[]{:S(2)}) %all-to-all-start) | async-done | bytes 64 | tf_op jit(solution)/shard_map/all_to_all | solution.py:40
  21.7 3.3 %all-to-all-start.1 = ((bf16[4,2,1024]{2,1,0:T(2,128)(2,1)}), bf16[4,2,1024]{2,1,0:T(2,128)(2,1)S(1)}, u32[]{:S(2)}, u32[]{:S(2)}) async-start(bf16[4,2,1024]{2,1,0:T(2,128)(2,1)} %reshape.759), calls=%async_computation.1 | async-start | bytes 32768 | tf_op jit(solution)/shard_map/all_to_all | solution.py:33
  25.0 0.5 broadcast.371
  25.5 0.7 reduce.12
  26.3 0.6 copy-done.3
  26.8 0.6 gather_fusion
  27.4 0.6 gather_fusion.2
  28.0 0.3 copy-done.1
  28.3 0.6 gather_fusion.1
  28.9 1.6 %all-to-all-done.1 = bf16[4,2,1024]{2,1,0:T(2,128)(2,1)S(1)} async-done(((bf16[4,2,1024]{2,1,0:T(2,128)(2,1)}), bf16[4,2,1024]{2,1,0:T(2,128)(2,1)S(1)}, u32[]{:S(2)}, u32[]{:S(2)}) %all-to-all-start.1) | async-done | bytes 16416 | tf_op jit(solution)/shard_map/all_to_all | solution.py:33
  30.5 0.1 reshape.760
  30.6 1.5 %sine_convert_fusion = (bf16[8,64,64]{2,1,0:T(8,128)(2,1)S(1)}, bf16[8,64,64]{2,1,0:T(8,128)(2,1)S(1)}) fusion(bf16[8,16,64]{2,1,0:T(8,128)(2,1)S(1)} %bitcast.151, f32[16,64]{1,0:T(8,128)S(1)} %copy-done.4), kind=kOutput, calls=%fused_computation.29 | convolution fusion | flops 6356992 | bytes 151552 | tf_op jit(solution)/shard_map/scn,cf->snf/dot_general | solution.py:88
  32.1 0.3 fusion.11
  32.4 0.2 multiply_convert_fusion
  32.6 0.2 fusion.40
  32.8 0.7 reshape.761
  33.5 4.0 %all-to-all-start.2 = ((f32[4,1,512]{2,1,0:T(1,128)}), f32[4,1,512]{2,1,0:T(1,128)S(1)}, u32[]{:S(2)}, u32[]{:S(2)}) async-start(f32[4,1,512]{2,1,0:T(1,128)} %reshape.761), calls=%async_computation.2 | async-start | bytes 16384 | tf_op jit(solution)/shard_map/all_to_all | solution.py:49
  37.5 5.6 %all-to-all-done.2 = f32[4,1,512]{2,1,0:T(1,128)S(1)} async-done(((f32[4,1,512]{2,1,0:T(1,128)}), f32[4,1,512]{2,1,0:T(1,128)S(1)}, u32[]{:S(2)}, u32[]{:S(2)}) %all-to-all-start.2) | async-done | bytes 8224 | tf_op jit(solution)/shard_map/all_to_all | solution.py:49
  43.1 0.5 broadcast.372
  43.6 0.7 reduce.13
  44.3 0.1 reshape.762
  44.4 0.6 gather_fusion.3
  45.0 0.3 reduce-window.14
  45.4 0.2 slice_reduce_fusion.1
  45.5 0.2 reduce-window.15
  45.8 0.1 reshape.674
  46.2 0.1 multiply_reduce_fusion
  46.3 0.5 copy-done.7
  46.8 0.5 copy-done.5
  47.4 0.1 reshape.675
  47.5 0.1 multiply_reduce_fusion.1
  47.6 1.3 %reduce-window.16 = f32[1,2,128]{2,1,0:T(2,128)S(1)} reduce-window(f32[1,2,128]{2,1,0:T(2,128)S(1)} %fusion.28, f32[]{:T(128)} %constant.68.clone.1), window={size=1x1x128 pad=0_0x0_0x0_127}, to_apply=%region_8.9 | reduce-window | flops 32512 | bytes 2052 | tf_op jit(solution)/shard_map/reduce-window.2
  48.9 0.1 slice_reduce_fusion
  49.2 0.2 reduce-window.19
  49.5 0.1 reshape.679
  49.7 0.6 scatter_fusion.1
  50.3 0.7 reshape.763
  51.0 3.2 %all-to-all-start.3 = ((bf16[4,1,512]{2,1,0:T(2,128)(2,1)}), bf16[4,1,512]{2,1,0:T(2,128)(2,1)S(1)}, u32[]{:S(2)}, u32[]{:S(2)}) async-start(bf16[4,1,512]{2,1,0:T(2,128)(2,1)} %reshape.763), calls=%async_computation.3 | async-start | bytes 16384 | tf_op jit(solution)/shard_map/all_to_all | solution.py:49
  54.4 5.4 %all-to-all-done.3 = bf16[4,1,512]{2,1,0:T(2,128)(2,1)S(1)} async-done(((bf16[4,1,512]{2,1,0:T(2,128)(2,1)}), bf16[4,1,512]{2,1,0:T(2,128)(2,1)S(1)}, u32[]{:S(2)}, u32[]{:S(2)}) %all-to-all-start.3) | async-done | bytes 4128 | tf_op jit(solution)/shard_map/all_to_all | solution.py:49
  59.8 0.5 broadcast.373
  60.4 0.7 reduce.14
  61.0 0.1 reshape.764
  61.1 0.1 convolution_bitcast_fusion.2
  61.3 0.2 fusion.1
  61.5 0.5 convolution_bitcast_fusion.1
  62.0 0.3 convolution_bitcast_fusion
  62.3 1.4 %fusion.4 = f32[4,128,128]{2,0,1:T(4,128)} fusion(f32[1,8,128,128]{3,2,1,0:T(8,128)S(1)} %convolution_bitcast_fusion.1, s32[8]{0:T(128)S(1)} %eq.47), kind=kOutput, calls=%fused_computation.18 | convolution fusion | flops 6291488 | bytes 786464 | tf_op jit(solution)/shard_map/dot_general | solution.py:60
  63.7 1.4 %fusion.2 = f32[4,128,128]{2,0,1:T(4,128)} fusion(f32[1,8,128,128]{3,2,1,0:T(8,128)S(1)} %convolution_bitcast_fusion, s32[8]{0:T(128)S(1)} %eq.47), kind=kOutput, calls=%fused_computation.15 | convolution fusion | flops 6291488 | bytes 786464 | tf_op jit(solution)/shard_map/dot_general | solution.py:60
  65.1 0.1 fusion.12
  65.2 5.8 %psum.23 = f32[4,4,128]{2,0,1:T(4,128)S(1)} all-reduce(f32[4,4,128]{2,0,1:T(4,128)S(1)} %fusion.12), channel_id=1, replica_groups=mesh['grp'=2,'brick'=4,'ray'=2,'rep'=2] {'ray','rep'}, use_global_device_ids=true, to_apply=%region_13.14 | all-reduce | flops 2048 | bytes 16384 | tf_op jit(solution)/shard_map/psum | solution.py:135
  71.1 0.6 copy.39
  71.7 25.0 %all-reduce.5.cloned.1.call-done = (f32[4,128,128]{2,0,1:T(4,128)}, f32[4,128,128]{2,0,1:T(4,128)}) async-done(((f32[4,128,128]{2,0,1:T(4,128)}, f32[4,128,128]{2,0,1:T(4,128)}), (f32[4,128,128]{2,0,1:T(4,128)}, f32[4,128,128]{2,0,1:T(4,128)})) %all-reduce.5.cloned.1.call-update) | async-done | bytes 524304 | tf_op jit(solution)/shard_map/psum | solution.py:135
  96.6 0.9 constant_dynamic-slice_fusion.1
  97.5 0.6 copy.38
  98.2 0.6 copy.37
  (44 shorter events, 1.4 us)
Async XLA Ops:
  7.2 20.2 %copy-start = (bf16[4,128,128]{2,1,0:T(8,128)(2,1)S(1)}, bf16[4,128,128]{2,1,0:T(8,128)(2,1)}, u32[]{:S(2)}) copy-start(bf16[4,128,128]{2,1,0:T(8,128)(2,1)} %param.10) | copy-start | bytes 393220
  8.0 0.7 copy-start.6
  9.9 11.8 %all-to-all-start = ((s32[4,1,2]{2,1,0:T(1,128)}), s32[4,1,2]{2,1,0:T(1,128)S(1)}, u32[]{:S(2)}, u32[]{:S(2)}) async-start(s32[4,1,2]{2,1,0:T(1,128)} %bitcast.4), calls=%async_computation | async-start | bytes 4096 | tf_op jit(solution)/shard_map/all_to_all | solution.py:40
  16.2 0.7 copy-start.2
  21.7 8.8 %all-to-all-start.1 = ((bf16[4,2,1024]{2,1,0:T(2,128)(2,1)}), bf16[4,2,1024]{2,1,0:T(2,128)(2,1)S(1)}, u32[]{:S(2)}, u32[]{:S(2)}) async-start(bf16[4,2,1024]{2,1,0:T(2,128)(2,1)} %reshape.759), calls=%async_computation.1 | async-start | bytes 32768 | tf_op jit(solution)/shard_map/all_to_all | solution.py:33
  26.1 0.7 copy-start.3
  27.4 0.9 copy-start.1
  28.9 1.7 %copy-start.4 = (f32[16,64]{1,0:T(8,128)S(1)}, f32[16,64]{1,0:T(8,128)}, u32[]{:S(2)}) copy-start(f32[16,64]{1,0:T(8,128)} %param.8) | copy-start | bytes 12292
  33.5 9.6 %all-to-all-start.2 = ((f32[4,1,512]{2,1,0:T(1,128)}), f32[4,1,512]{2,1,0:T(1,128)S(1)}, u32[]{:S(2)}, u32[]{:S(2)}) async-start(f32[4,1,512]{2,1,0:T(1,128)} %reshape.761), calls=%async_computation.2 | async-start | bytes 16384 | tf_op jit(solution)/shard_map/all_to_all | solution.py:49
  46.2 0.7 copy-start.7
  46.8 0.5 copy-start.5
  51.0 8.8 %all-to-all-start.3 = ((bf16[4,1,512]{2,1,0:T(2,128)(2,1)}), bf16[4,1,512]{2,1,0:T(2,128)(2,1)S(1)}, u32[]{:S(2)}, u32[]{:S(2)}) async-start(bf16[4,1,512]{2,1,0:T(2,128)(2,1)} %reshape.763), calls=%async_computation.3 | async-start | bytes 16384 | tf_op jit(solution)/shard_map/all_to_all | solution.py:49
  54.3 42.4 %all-reduce.5.cloned.1.call-start = ((), (), s32[]{:S(2)}) async-start(), calls=%async_computation.4 | async-start | bytes 1048576 | tf_op jit(solution)/shard_map/psum | solution.py:135
Sparse Core Ops, SparseCore 0:
  65.2 31.4 all-reduce.4
where the time goes:
time: 106 us
  waiting for transfers between devices  41 us (39%)
  starting transfers between devices  16.9 us (16%)
  local copies, waits for them, and re-layouts  16.2 us (15%)
  between operations  14.3 us (13%)
  matrix products  6.12 us (6%)
  blocking collectives  5.8 us (5%)
  other arithmetic  5.41 us (5%)
    psum x1, waiting for transfers between devices, on_device(): lax.psum((grad_first, grad_second, grad_last), ('ray', 'rep'))  25 us
    all_to_all x2, waiting for transfers between devices, trade_rows(): lax.all_to_all(rows_in.reshape((owners, CAP) + rows_in.shape[1:]), 'brick...  11 us
    unnamed x25, local copies, waits for them, and re-layouts  7.35 us
    all_to_all x2, starting transfers between devices, trade_rows(): lax.all_to_all(rows_in.reshape((owners, CAP) + rows_in.shape[1:]), 'brick...  7.27 us
    all_to_all x1, starting transfers between devices, send_blocks(): lax.all_to_all(labels.reshape(owners, CAP), 'brick', split_axis=0, concat...  6.32 us
    psum x1, blocking collectives, on_device(): lax.psum((grad_first, grad_second, grad_last), ('ray', 'rep'))  5.8 us
    all_to_all x1, waiting for transfers between devices, send_blocks(): lax.all_to_all(labels.reshape(owners, CAP), 'brick', split_axis=0, concat...  3.41 us
    all_to_all x1, starting transfers between devices, send_blocks(): lax.all_to_all(outgoing.reshape((owners, CAP) + outgoing.shape[1:]), 'bri...  3.25 us
  transfers between devices with their start and end apart: 5, of which 5 were waited for; matrix products, arithmetic and copies ran while one was open for 5% of the time, Pallas kernels for 0%

commit v1 on v0

--- a/solution.py
+++ b/solution.py
@@ -1,6 +1,10 @@
+import functools
+
 import jax
 import jax.numpy as jnp
 from jax import lax
+from jax.experimental import pallas as pl
+from jax.experimental.pallas import tpu as pltpu
 from jax.sharding import PartitionSpec as P
 
 CAP = 2
@@ -63,7 +67,7 @@
     return summed.reshape((brick_table.shape[1],) + slot_terms.shape[1:])
 
 
-def on_device(samples, frequencies, w_first, w_second, w_out, brick_ids, targets):
+def layered_plan(samples, frequencies, w_first, w_second, w_out, brick_ids, targets):
     ray_rows, blocks_per_ray, channels, length = samples.shape
     bricks_here = w_first.shape[0]
     owners = lax.axis_size("brick")
@@ -143,6 +147,461 @@
     grad_second = lax.dynamic_slice_in_dim(grad_second, group_index * hidden_share, hidden_share, 1)
     grad_last = lax.dynamic_slice_in_dim(grad_last, group_index * hidden_share, hidden_share, 2)
     return (predicted, grad_first, grad_second, grad_last)
+
+
+F32 = jnp.float32
+BF16 = jnp.bfloat16
+MESH = pl.DeviceIdType.MESH
+
+
+def split3(values):
+    high = values.astype(BF16)
+    rest = values - high.astype(F32)
+    middle = rest.astype(BF16)
+    low = (rest - middle.astype(F32)).astype(BF16)
+    return high, middle, low
+
+
+def nn(left, right):
+    return jnp.dot(left, right, preferred_element_type=F32)
+
+
+def nt(left, right):
+    return lax.dot_general(left, right, (((1,), (1,)), ((), ())), preferred_element_type=F32)
+
+
+def sin_cos(phases, half):
+    turns = jnp.floor(phases * 0.3183098861837907 + (half + 0.5))
+    shift = turns - half
+    rest = phases - shift * 3.140625
+    rest = rest - shift * 9.67502593994140625e-4
+    rest = rest - shift * 1.509957990978376432e-7
+    half_turns = turns * 0.5
+    sign = 1.0 - 4.0 * (half_turns - jnp.floor(half_turns))
+    square = rest * rest
+    poly = -2.3889859e-08
+    for factor in (2.7525562e-06, -0.00019840874, 0.0083333310, -0.16666667):
+        poly = poly * square + factor
+    return (rest + rest * square * poly) * sign
+
+
+def softplus(values):
+    decay = jnp.exp(-jnp.abs(values))
+    ratio = decay / (2.0 + decay)
+    square = ratio * ratio
+    poly = jnp.full_like(values, 1.0 / 17.0)
+    for order in (15, 13, 11, 9, 7, 5, 3, 1):
+        poly = poly * square + 1.0 / order
+    return jnp.maximum(values, 0.0) + 2.0 * ratio * poly
+
+
+def one_minus_exp(values, decay):
+    series = jnp.full_like(values, 1.0)
+    for order in (8, 7, 6, 5, 4, 3, 2):
+        series = 1.0 - values * (1.0 / order) * series
+    return jnp.where(values < 0.5, values * series, 1.0 - decay)
+
+
+def fused_kernel(
+    owners,
+    rays,
+    reps,
+    ids_ref,
+    targets_ref,
+    samples_ref,
+    freq_ref,
+    w1_ref,
+    w2_ref,
+    wo_ref,
+    pred_ref,
+    gf_ref,
+    gs_ref,
+    go_ref,
+    sx,
+    rx,
+    sf,
+    rf,
+    sg,
+    rg,
+    enc_s,
+    h1_s,
+    h2_s,
+    slope1_s,
+    slope2_s,
+    sx_send,
+    sx_recv,
+    relay_send,
+    relay_recv,
+    sf_send,
+    sf_recv,
+    sg_send,
+    sg_recv,
+):
+    bricks, features, hidden = w1_ref.shape
+    channels_out = wo_ref.shape[1]
+    blocks, channels, length = samples_ref.shape[1:]
+    groups = rays * reps
+    wide = owners * CAP * length
+    pair = CAP * length
+    share = features // groups
+    my_owner = lax.axis_index("brick")
+    my_group = lax.axis_index("ray") * reps + lax.axis_index("rep")
+
+    def device(owner_step, group_step):
+        group = lax.rem(my_group + group_step, groups)
+        return {
+            "brick": lax.rem(my_owner + owner_step, owners),
+            "ray": group // reps,
+            "rep": lax.rem(group, reps),
+        }
+
+    barrier = pltpu.get_barrier_semaphore()
+    for d in range(groups):
+        for e in range(owners):
+            if d or e:
+                pl.semaphore_signal(barrier, inc=1, device_id=device(e, d), device_id_type=MESH)
+
+    ids = [ids_ref[0, k] for k in range(blocks)]
+    owner_of = [lax.div(i, bricks) for i in ids]
+    local = [(ids[k] - owner_of[k] * bricks).astype(F32) for k in range(blocks)]
+    rank = []
+    for k in range(blocks):
+        earlier = jnp.int32(0)
+        for j in range(k):
+            earlier = earlier + jnp.where(owner_of[j] == owner_of[k], 1, 0)
+        rank.append(earlier)
+    at_step = [lax.rem(my_owner + e, owners) for e in range(owners)]
+
+    def chosen(k, e, c):
+        return jnp.where(owner_of[k] == at_step[e], jnp.where(rank[k] == c, 1, 0), 0)
+
+    picks = [
+        [[chosen(k, e, c).astype(F32) for c in range(CAP)] for e in range(owners)]
+        for k in range(blocks)
+    ]
+    tiles = [samples_ref[0, k].astype(F32) for k in range(blocks)]
+    for e in range(owners):
+        parts = []
+        labels = []
+        for c in range(CAP):
+            block = jnp.zeros((channels, length), F32)
+            label = jnp.float32(bricks)
+            for k in range(blocks):
+                block = block + picks[k][e][c] * tiles[k]
+                label = label + picks[k][e][c] * (local[k] - bricks)
+            parts.append(block)
+            labels.append(jnp.full((16, length), label, F32))
+        sx[e, :channels, :] = jnp.concatenate(parts, axis=1).astype(BF16)
+        sx[e, channels:, :] = jnp.concatenate(labels, axis=1).astype(BF16)
+    rx[0, 0] = sx[0]
+
+    pl.semaphore_wait(barrier, owners * groups - 1)
+
+    started = []
+    first = []
+    for e in range(1, owners):
+        copy = pltpu.make_async_remote_copy(
+            src_ref=sx.at[e],
+            dst_ref=rx.at[0, e],
+            send_sem=sx_send.at[e],
+            recv_sem=sx_recv.at[e],
+            device_id=device(e, 0),
+            device_id_type=MESH,
+        )
+        copy.start()
+        first.append(copy)
+
+    freq = freq_ref[...]
+    stacked = jnp.concatenate([part.astype(F32) for part in split3(freq)], axis=0)
+    freq_t = jnp.concatenate([stacked, stacked], axis=1).T.astype(BF16)
+    w1_t = jnp.concatenate(
+        [w1_ref[b].astype(F32).T.astype(BF16) for b in range(bricks)], axis=1
+    )
+    w2_t = jnp.concatenate(
+        [w2_ref[b].astype(F32).T.astype(BF16) for b in range(bricks)], axis=1
+    )
+    w2_cat = jnp.concatenate([w2_ref[b] for b in range(bricks)], axis=1)
+    wo_rows = jnp.concatenate(
+        [wo_ref[b].astype(F32) for b in range(bricks)], axis=0
+    )
+    wo_cat = wo_rows.astype(BF16)
+    wo_t = wo_rows.T.astype(BF16)
+    half = jnp.where(
+        lax.broadcasted_iota(jnp.int32, (features, wide), 0) < features // 2, 0.0, 0.5
+    ).astype(F32)
+    brick_row = (
+        lax.broadcasted_iota(jnp.int32, (bricks * channels_out, wide), 0) // channels_out
+    ).astype(F32)
+
+    for copy in first:
+        copy.wait_recv()
+        started.append(copy)
+    relays = []
+    for d in range(1, groups):
+        copy = pltpu.make_async_remote_copy(
+            src_ref=rx.at[0],
+            dst_ref=rx.at[d],
+            send_sem=relay_send.at[d],
+            recv_sem=relay_recv.at[d],
+            device_id=device(0, d),
+            device_id_type=MESH,
+        )
+        copy.start()
+        relays.append(copy)
+        started.append(copy)
+
+    def label_tile(d):
+        return jnp.concatenate(
+            [rx[d, e, channels:, :].astype(F32) for e in range(owners)], axis=1
+        )
+
+    def masks(d):
+        labels = label_tile(d)
+        return [jnp.where(labels == b, 1.0, 0.0).astype(BF16) for b in range(bricks)]
+
+    def masked(values, mask):
+        copies = values.shape[0] // 16
+        return jnp.concatenate(
+            [values * jnp.concatenate([m] * copies, axis=0) for m in mask], axis=0
+        )
+
+    def forward(d):
+        mask = masks(d)
+        rows = jnp.concatenate([rx[d, e, :channels, :] for e in range(owners)], axis=1)
+        phases = nn(freq_t, jnp.concatenate([rows] * 3, axis=0))
+        encoded = sin_cos(phases, half).astype(BF16)
+        enc_s[d] = encoded
+        pre = nn(w1_t, masked(encoded, mask))
+        squashed = 1.0 / (1.0 + jnp.exp(-pre))
+        value = pre * squashed
+        h1 = value.astype(BF16)
+        h1_s[d] = h1
+        slope1_s[d] = squashed + value * (1.0 - squashed)
+        pre = nn(w2_t, masked(h1, mask))
+        squashed = 1.0 / (1.0 + jnp.exp(-pre))
+        value = pre * squashed
+        h2 = value.astype(BF16)
+        h2_s[d] = h2
+        slope2_s[d] = squashed + value * (1.0 - squashed)
+        return h2
+
+    h2 = forward(0)
+    by_brick = nn(wo_cat, h2)
+    labels = label_tile(0)
+    field = jnp.zeros((channels_out, wide), F32)
+    for b in range(bricks):
+        rows = by_brick[b * channels_out : (b + 1) * channels_out]
+        field = field + jnp.where(labels[:channels_out] == b, rows, 0.0)
+    field = jnp.concatenate([field, jnp.zeros((8 - channels_out, wide), F32)], axis=0)
+    for e in range(owners):
+        sf[e] = field[:, e * pair : (e + 1) * pair]
+    rf[0] = sf[0]
+    fields = []
+    for e in range(1, owners):
+        copy = pltpu.make_async_remote_copy(
+            src_ref=sf.at[e],
+            dst_ref=rf.at[e],
+            send_sem=sf_send.at[e],
+            recv_sem=sf_recv.at[e],
+            device_id=device(owners - e, 0),
+            device_id_type=MESH,
+        )
+        copy.start()
+        fields.append(copy)
+        started.append(copy)
+
+    for d in range(1, groups):
+        relays[d - 1].wait_recv()
+        forward(d)
+
+    for copy in fields:
+        copy.wait_recv()
+
+    lane = lax.broadcasted_iota(jnp.int32, (8, pair), 1)
+    got = [rf[e] for e in range(owners)]
+    swapped = [
+        jnp.concatenate([piece[:, length:], piece[:, :length]], axis=1) for piece in got
+    ]
+    pairs = []
+    for p in range(blocks // CAP):
+        halves = []
+        for c in range(CAP):
+            k = p * CAP + c
+            total = jnp.zeros((8, pair), F32)
+            for e in range(owners):
+                total = total + picks[k][e][c] * got[e] + picks[k][e][1 - c] * swapped[e]
+            halves.append(total)
+        pairs.append(jnp.where(lane < length, halves[0], halves[1]))
+    rows = len(pairs)
+    channel = [
+        jnp.concatenate([one[o : o + 1] for one in pairs], axis=0) for o in range(channels_out)
+    ]
+    row_of = lax.broadcasted_iota(jnp.int32, (pair, pair), 0)
+    column_of = lax.broadcasted_iota(jnp.int32, (pair, pair), 1)
+    upper = jnp.where(row_of < column_of, 1.0, 0.0).astype(BF16)
+    lower = jnp.where(row_of > column_of, 1.0, 0.0).astype(BF16)
+
+    def summed(values, triangle):
+        high, middle, low = split3(values)
+        return nn(high, triangle) + nn(middle, triangle) + nn(low, triangle)
+
+    def offsets(values, reverse):
+        totals = jnp.sum(values, axis=1, keepdims=True)
+        kept = [jnp.zeros((1, 1), F32)]
+        order = range(rows - 1, 0, -1) if reverse else range(rows - 1)
+        for r in order:
+            kept.append(kept[-1] + totals[r : r + 1])
+        return jnp.concatenate(kept[::-1] if reverse else kept, axis=0)
+
+    optical = softplus(channel[0]) * (1.0 / length)
+    before = summed(optical, upper) + offsets(optical, False)
+    through = jnp.exp(-before)
+    decay = jnp.exp(-optical)
+    weights = through * one_minus_exp(optical, decay)
+    pull = []
+    lifted = jnp.zeros((rows, pair), F32)
+    for c in range(channels_out - 1):
+        signal = channel[c + 1]
+        predicted = jnp.sum(
+            jnp.sum(weights * signal, axis=1, keepdims=True), axis=0, keepdims=True
+        )
+        pred_ref[c : c + 1, :] = predicted
+        miss = loss_scale * (predicted - targets_ref[c, 0])
+        pull.append(miss * weights)
+        lifted = lifted + miss * signal
+    product = lifted * weights
+    after = summed(product, lower) + offsets(product, True)
+    density_grad = (
+        (lifted * through * decay - after) * (1.0 / length) / (1.0 + jnp.exp(-channel[0]))
+    )
+    grads = [density_grad] + pull
+    grad_pairs = []
+    for p in range(rows):
+        rows4 = jnp.concatenate([g[p : p + 1] for g in grads], axis=0)
+        grad_pairs.append(jnp.concatenate([rows4] * (8 // channels_out), axis=0))
+    grad_swapped = [
+        jnp.concatenate([piece[:, length:], piece[:, :length]], axis=1) for piece in grad_pairs
+    ]
+    for e in range(owners):
+        halves = []
+        for c in range(CAP):
+            total = jnp.zeros((8, pair), F32)
+            for k in range(blocks):
+                source = grad_pairs if k % CAP == c else grad_swapped
+                total = total + picks[k][e][c] * source[k // CAP]
+            halves.append(total)
+        tile = jnp.where(lane < length, halves[0], halves[1])
+        sg[e] = jnp.concatenate([tile, tile], axis=0).astype(BF16)
+    rg[0, 0] = sg[0]
+    arriving = [[] for _ in range(groups)]
+    for d in range(groups):
+        for e in range(owners):
+            if d or e:
+                copy = pltpu.make_async_remote_copy(
+                    src_ref=sg.at[e],
+                    dst_ref=rg.at[d, e],
+                    send_sem=sg_send.at[d, e],
+                    recv_sem=sg_recv.at[d, e],
+                    device_id=device(e, d),
+                    device_id_type=MESH,
+                )
+                copy.start()
+                arriving[d].append(copy)
+                started.append(copy)
+
+    mine = pl.ds(pl.multiple_of(my_group * share, share), share)
+    gf = jnp.zeros((bricks * share, hidden), F32)
+    gs = jnp.zeros((bricks * share, hidden), F32)
+    go = jnp.zeros((bricks * channels_out, share), F32)
+    for d in range(groups):
+        mask = masks(d)
+        for copy in arriving[d]:
+            copy.wait_recv()
+        rows16 = jnp.concatenate([rg[d, e] for e in range(owners)], axis=1)
+        rows16 = rows16 * jnp.where(label_tile(d) == brick_row, 1.0, 0.0).astype(BF16)
+        d2 = (nn(wo_t, rows16) * slope2_s[d]).astype(BF16)
+        d1 = (nn(w2_cat, masked(d2, mask)) * slope1_s[d]).astype(BF16)
+        gs = gs + nt(masked(h1_s[d, mine, :], mask), d2)
+        go = go + nt(rows16, h2_s[d, mine, :])
+        gf = gf + nt(masked(enc_s[d, mine, :], mask), d1)
+    for b in range(bricks):
+        gf_ref[b] = gf[b * share : (b + 1) * share]
+        gs_ref[b] = gs[b * share : (b + 1) * share]
+        go_ref[b] = go[b * channels_out : (b + 1) * channels_out]
+
+    for copy in started:
+        copy.wait_send()
+
+
+def fused_plan(samples, frequencies, w_first, w_second, w_out, brick_ids, targets):
+    owners = lax.axis_size("brick")
+    rays = lax.axis_size("ray")
+    reps = lax.axis_size("rep")
+    groups = rays * reps
+    bricks, features, hidden = w_first.shape
+    out = w_out.shape[1]
+    length = samples.shape[3]
+    pair = CAP * length
+    wide = owners * pair
+    share = features // groups
+    vmem = pl.BlockSpec(memory_space=pltpu.VMEM)
+    smem = pl.BlockSpec(memory_space=pltpu.SMEM)
+    dma = pltpu.SemaphoreType.DMA
+    return pl.pallas_call(
+        functools.partial(fused_kernel, owners, rays, reps),
+        out_shape=(
+            jax.ShapeDtypeStruct(targets.shape, F32),
+            jax.ShapeDtypeStruct((bricks, share, hidden), F32),
+            jax.ShapeDtypeStruct((bricks, share, hidden), F32),
+            jax.ShapeDtypeStruct((bricks, out, share), F32),
+        ),
+        in_specs=[smem, smem, vmem, vmem, vmem, vmem, vmem],
+        out_specs=(vmem, vmem, vmem, vmem),
+        scratch_shapes=[
+            pltpu.VMEM((owners, 32, pair), BF16),
+            pltpu.VMEM((groups, owners, 32, pair), BF16),
+            pltpu.VMEM((owners, 8, pair), F32),
+            pltpu.VMEM((owners, 8, pair), F32),
+            pltpu.VMEM((owners, 16, pair), BF16),
+            pltpu.VMEM((groups, owners, 16, pair), BF16),
+            pltpu.VMEM((groups, features, wide), BF16),
+            pltpu.VMEM((groups, hidden, wide), BF16),
+            pltpu.VMEM((groups, hidden, wide), BF16),
+            pltpu.VMEM((groups, hidden, wide), F32),
+            pltpu.VMEM((groups, hidden, wide), F32),
+            dma((owners,)),
+            dma((owners,)),
+            dma((groups,)),
+            dma((groups,)),
+            dma((owners,)),
+            dma((owners,)),
+            dma((groups, owners)),
+            dma((groups, owners)),
+        ],
+        compiler_params=pltpu.CompilerParams(
+            collective_id=0, has_side_effects=True, vmem_limit_bytes=40 * 1024 * 1024
+        ),
+    )(brick_ids, targets, samples, frequencies, w_first, w_second, w_out)
+
+
+def on_device(samples, frequencies, w_first, w_second, w_out, brick_ids, targets):
+    owners = lax.axis_size("brick")
+    groups = lax.axis_size(("ray", "rep"))
+    bricks, features, hidden = w_first.shape
+    ray_rows, blocks, channels, length = samples.shape
+    fits = (
+        ray_rows == 1
+        and blocks % CAP == 0
+        and CAP == 2
+        and CAP * length == 128
+        and channels == 16
+        and bricks * w_out.shape[1] == 16
+        and features == hidden
+        and features % (16 * groups) == 0
+        and groups * owners <= 16
+    )
+    plan = fused_plan if fits else layered_plan
+    return plan(samples, frequencies, w_first, w_second, w_out, brick_ids, targets)
 
 
 def solution(mesh):

time: 106 us -> 29.7 us (0.28)
  waiting for transfers between devices: 41 us -> 0 us
  Pallas kernels: 0 us -> 21.5 us
  starting transfers between devices: 16.9 us -> 0 us
  between operations: 14.3 us -> 0.65 us
  local copies, waits for them, and re-layouts: 16.2 us -> 7.11 us
  matrix products: 6.12 us -> 0 us
  blocking collectives: 5.8 us -> 0 us
  other arithmetic: 5.41 us -> 0 us
    psum x1 -> x0, waiting for transfers between devices: 25 us -> none  [on_device(): lax.psum((grad_first, grad_second, grad_last), ('ray', 'rep'))]
    pallas_call x0 -> x1, Pallas kernels: none -> 21.5 us  [fused_plan(): pl.pallas_call(functools.partial(fused_kernel, owners, rays, reps), out_s...]
    all_to_all x4 -> x0, starting transfers between devices: 16.8 us -> none  [the longest x2 7.27 us: trade_rows(): lax.all_to_all(rows_in.reshape((owners, CAP) + rows_in.shape[1:]), 'brick...]
    all_to_all x4 -> x0, waiting for transfers between devices: 16 us -> none  [the longest x2 11 us: trade_rows(): lax.all_to_all(rows_in.reshape((owners, CAP) + rows_in.shape[1:]), 'brick...]
    dot_general x11 -> x0, matrix products: 6.12 us -> none  [the longest x3 2.85 us: per_brick(): jnp.dot(brick_table.T, slot_terms.reshape(slot_terms.shape[0], -1), preci...]
    psum x1 -> x0, blocking collectives: 5.8 us -> none  [on_device(): lax.psum((grad_first, grad_second, grad_last), ('ray', 'rep'))]
    gather x5 -> x0, local copies, waits for them, and re-layouts: 2.34 us -> none  [the longest x1 0.6 us: on_device(): second = w_second[in_labels]]
    all_to_all x4 -> x0, local copies, waits for them, and re-layouts: 2.2 us -> none  [the longest x2 1.17 us: send_blocks(): lax.all_to_all(labels.reshape(owners, CAP), 'brick', split_axis=0, concat...]
  transfers between devices with their start and end apart: 5 -> 0, of which waited for: 5 -> 0; matrix products, arithmetic and copies ran while one was open for 5% -> 0% of each run, Pallas kernels for 0% -> 0%
where the time goes in v1:
time: 29.7 us; the launch traced here: 29.3 us
  Pallas kernels  21.5 us (72%)
  local copies, waits for them, and re-layouts  7.11 us (24%)
  between operations  0.65 us (2%)
    pallas_call x1, Pallas kernels, fused_plan(): pl.pallas_call(functools.partial(fused_kernel, owners, rays, reps), out_s...  21.5 us
    unnamed x16, local copies, waits for them, and re-layouts  6.51 us
    pallas_call x1, local copies, waits for them, and re-layouts, fused_plan(): pl.pallas_call(functools.partial(fused_kernel, owners, rays, reps), out_s...  0.6 us

profile of v1, /device:TPU:0, one launch (start us, length us, event | category | flops | bytes accessed | tf_op | source)
XLA Modules:
  0.0 29.3 jit_solution(13688724627699805413)
XLA Ops:
  0.6 0.0 copy-start.5
  0.6 0.7 %copy.11.targets_ref = f32[3,1]{1,0:T(4,128)S(1)} copy(f32[3,1]{0,1:T(1,128)} %param.13) | data formatting | bytes 24 | tf_op args[6]
  1.4 0.0 copy-done.5
  1.4 0.0 copy-start
  1.4 0.9 %copy-done = bf16[4,128,128]{2,1,0:T(8,128)(2,1)S(1)} copy-done((bf16[4,128,128]{2,1,0:T(8,128)(2,1)S(1)}, bf16[4,128,128]{2,1,0:T(8,128)(2,1)}, u32[]{:S(2)}) %copy-start) | copy-done | bytes 131096
  2.3 0.0 copy-start.1
  2.3 0.9 %copy-done.1 = bf16[4,128,128]{2,1,0:T(8,128)(2,1)S(1)} copy-done((bf16[4,128,128]{2,1,0:T(8,128)(2,1)S(1)}, bf16[4,128,128]{2,1,0:T(8,128)(2,1)}, u32[]{:S(2)}) %copy-start.1) | copy-done | bytes 131096
  3.2 0.0 copy-start.2
  3.2 0.7 %copy-done.2 = bf16[1,4,16,64]{3,2,1,0:T(8,128)(2,1)S(1)} copy-done((bf16[1,4,16,64]{3,2,1,0:T(8,128)(2,1)S(1)}, bf16[1,4,16,64]{3,2,1,0:T(8,128)(2,1)}, u32[]{:S(2)}) %copy-start.2) | copy-done | bytes 8216
  3.9 0.0 copy-start.3
  3.9 0.7 %copy-done.3 = f32[16,64]{1,0:T(8,128)S(1)} copy-done((f32[16,64]{1,0:T(8,128)S(1)}, f32[16,64]{1,0:T(8,128)}, u32[]{:S(2)}) %copy-start.3) | copy-done | bytes 4120
  4.6 0.0 copy-start.4
  4.6 0.7 %copy-done.4 = bf16[4,4,128]{2,1,0:T(4,128)(2,1)S(1)} copy-done((bf16[4,4,128]{2,1,0:T(4,128)(2,1)S(1)}, bf16[4,4,128]{2,1,0:T(4,128)(2,1)}, u32[]{:S(2)}) %copy-start.4) | copy-done | bytes 4120
  5.3 21.5 %shard_map.102 = (f32[3,1]{1,0:T(4,128)S(1)}, f32[4,32,128]{2,1,0:T(8,128)S(1)}, f32[4,32,128]{2,1,0:T(8,128)S(1)}, f32[4,4,32]{2,1,0:T(4,128)S(1)}) custom-call(s32[1,4]{1,0:T(1,128)S(1)} %copy-done.5, f32[3,1]{1,0:T(4,128)S(1)} %copy.11.targets_ref, bf16[1,4,16,64]{3,2,1,0:T(8,128)(2,1)S(1)} %copy-done.2, f32[16,64]{1,0:T(8,128)S(1)} %copy-done.3, ...), custom_call_target="tpu_custom_call" | custom-call | tf_op jit(solution)/shard_map/pallas_call | solution.py:550
  26.9 0.6 %copy.12 = f32[3,1]{0,1:T(1,128)} copy(f32[3,1]{1,0:T(4,128)S(1)} %get-tuple-element.4) | data formatting | bytes 24 | tf_op jit(solution)/shard_map/pallas_call | solution.py:550
  27.5 0.6 %copy.16 = f32[4,32,128]{2,1,0:T(8,128)} copy(f32[4,32,128]{2,1,0:T(8,128)S(1)} %get-tuple-element.13) | data formatting | bytes 131072
  28.1 0.6 %copy.17 = f32[4,32,128]{2,1,0:T(8,128)} copy(f32[4,32,128]{2,1,0:T(8,128)S(1)} %get-tuple-element.14) | data formatting | bytes 131072
  28.7 0.6 %copy.18 = f32[4,4,32]{2,1,0:T(4,128)} copy(f32[4,4,32]{2,1,0:T(4,128)S(1)} %get-tuple-element.15) | data formatting | bytes 4096
Async XLA Ops:
  0.6 0.8 %copy-start.5 = (s32[1,4]{1,0:T(1,128)S(1)}, s32[1,4]{1,0:T(1,128)}, u32[]{:S(2)}) copy-start(s32[1,4]{1,0:T(1,128)} %ids_ref.1) | copy-start | bytes 52
  1.4 0.9 %copy-start = (bf16[4,128,128]{2,1,0:T(8,128)(2,1)S(1)}, bf16[4,128,128]{2,1,0:T(8,128)(2,1)}, u32[]{:S(2)}) copy-start(bf16[4,128,128]{2,1,0:T(8,128)(2,1)} %w1_ref.1) | copy-start | bytes 393220
  2.3 0.9 %copy-start.1 = (bf16[4,128,128]{2,1,0:T(8,128)(2,1)S(1)}, bf16[4,128,128]{2,1,0:T(8,128)(2,1)}, u32[]{:S(2)}) copy-start(bf16[4,128,128]{2,1,0:T(8,128)(2,1)} %w2_ref.1) | copy-start | bytes 393220
  3.2 0.7 %copy-start.2 = (bf16[1,4,16,64]{3,2,1,0:T(8,128)(2,1)S(1)}, bf16[1,4,16,64]{3,2,1,0:T(8,128)(2,1)}, u32[]{:S(2)}) copy-start(bf16[1,4,16,64]{3,2,1,0:T(8,128)(2,1)} %samples_ref.1) | copy-start | bytes 24580
  3.9 0.7 %copy-start.3 = (f32[16,64]{1,0:T(8,128)S(1)}, f32[16,64]{1,0:T(8,128)}, u32[]{:S(2)}) copy-start(f32[16,64]{1,0:T(8,128)} %freq_ref.1) | copy-start | bytes 12292
  4.6 0.7 %copy-start.4 = (bf16[4,4,128]{2,1,0:T(4,128)(2,1)S(1)}, bf16[4,4,128]{2,1,0:T(4,128)(2,1)}, u32[]{:S(2)}) copy-start(bf16[4,4,128]{2,1,0:T(4,128)(2,1)} %wo_ref.1) | copy-start | bytes 12292

commit v2 on v1

--- a/solution.py
+++ b/solution.py
@@ -149,6 +149,7 @@
     return (predicted, grad_first, grad_second, grad_last)
 
 
+EARLY = 2
 F32 = jnp.float32
 BF16 = jnp.bfloat16
 MESH = pl.DeviceIdType.MESH
@@ -208,11 +209,11 @@
     reps,
     ids_ref,
     targets_ref,
-    samples_ref,
-    freq_ref,
-    w1_ref,
-    w2_ref,
-    wo_ref,
+    samples_hbm,
+    freq_hbm,
+    w1_hbm,
+    w2_hbm,
+    wo_hbm,
     pred_ref,
     gf_ref,
     gs_ref,
@@ -223,11 +224,17 @@
     rf,
     sg,
     rg,
+    samples_ref,
+    freq_ref,
+    w1_ref,
+    w2_ref,
+    wo_ref,
     enc_s,
     h1_s,
     h2_s,
     slope1_s,
     slope2_s,
+    load_sem,
     sx_send,
     sx_recv,
     relay_send,
@@ -255,6 +262,20 @@
             "rep": lax.rem(group, reps),
         }
 
+    loads = [
+        pltpu.make_async_copy(source, target, load_sem.at[i])
+        for i, (source, target) in enumerate(
+            (
+                (samples_hbm, samples_ref),
+                (freq_hbm, freq_ref),
+                (w1_hbm, w1_ref),
+                (w2_hbm, w2_ref),
+                (wo_hbm, wo_ref),
+            )
+        )
+    ]
+    for load in loads:
+        load.start()
     barrier = pltpu.get_barrier_semaphore()
     for d in range(groups):
         for e in range(owners):
@@ -279,6 +300,7 @@
         [[chosen(k, e, c).astype(F32) for c in range(CAP)] for e in range(owners)]
         for k in range(blocks)
     ]
+    loads[0].wait()
     tiles = [samples_ref[0, k].astype(F32) for k in range(blocks)]
     for e in range(owners):
         parts = []
@@ -311,6 +333,8 @@
         copy.start()
         first.append(copy)
 
+    for load in loads[1:]:
+        load.wait()
     freq = freq_ref[...]
     stacked = jnp.concatenate([part.astype(F32) for part in split3(freq)], axis=0)
     freq_t = jnp.concatenate([stacked, stacked], axis=1).T.astype(BF16)
@@ -372,13 +396,13 @@
         encoded = sin_cos(phases, half).astype(BF16)
         enc_s[d] = encoded
         pre = nn(w1_t, masked(encoded, mask))
-        squashed = 1.0 / (1.0 + jnp.exp(-pre))
+        squashed = 0.5 + 0.5 * jnp.tanh(0.5 * pre)
         value = pre * squashed
         h1 = value.astype(BF16)
         h1_s[d] = h1
         slope1_s[d] = squashed + value * (1.0 - squashed)
         pre = nn(w2_t, masked(h1, mask))
-        squashed = 1.0 / (1.0 + jnp.exp(-pre))
+        squashed = 0.5 + 0.5 * jnp.tanh(0.5 * pre)
         value = pre * squashed
         h2 = value.astype(BF16)
         h2_s[d] = h2
@@ -410,7 +434,7 @@
         fields.append(copy)
         started.append(copy)
 
-    for d in range(1, groups):
+    for d in range(1, EARLY):
         relays[d - 1].wait_recv()
         forward(d)
 
@@ -459,16 +483,18 @@
     decay = jnp.exp(-optical)
     weights = through * one_minus_exp(optical, decay)
     pull = []
+    predictions = []
     lifted = jnp.zeros((rows, pair), F32)
     for c in range(channels_out - 1):
         signal = channel[c + 1]
         predicted = jnp.sum(
             jnp.sum(weights * signal, axis=1, keepdims=True), axis=0, keepdims=True
         )
-        pred_ref[c : c + 1, :] = predicted
-        miss = loss_scale * (predicted - targets_ref[c, 0])
+        predictions.append(predicted)
+        miss = loss_scale * (predicted - targets_ref[0, c])
         pull.append(miss * weights)
         lifted = lifted + miss * signal
+    pred_ref[...] = jnp.concatenate(predictions, axis=1)
     product = lifted * weights
     after = summed(product, lower) + offsets(product, True)
     density_grad = (
@@ -509,6 +535,10 @@
                 arriving[d].append(copy)
                 started.append(copy)
 
+    for d in range(EARLY, groups):
+        relays[d - 1].wait_recv()
+        forward(d)
+
     mine = pl.ds(pl.multiple_of(my_group * share, share), share)
     gf = jnp.zeros((bricks * share, hidden), F32)
     gs = jnp.zeros((bricks * share, hidden), F32)
@@ -533,6 +563,18 @@
         copy.wait_send()
 
 
+def place_kernel(*refs):
+    sources, targets, sem = refs[:4], refs[4:8], refs[8]
+    copies = [
+        pltpu.make_async_copy(source, target, sem.at[i])
+        for i, (source, target) in enumerate(zip(sources, targets))
+    ]
+    for copy in copies:
+        copy.start()
+    for copy in copies:
+        copy.wait()
+
+
 def fused_plan(samples, frequencies, w_first, w_second, w_out, brick_ids, targets):
     owners = lax.axis_size("brick")
     rays = lax.axis_size("ray")
@@ -546,16 +588,17 @@
     share = features // groups
     vmem = pl.BlockSpec(memory_space=pltpu.VMEM)
     smem = pl.BlockSpec(memory_space=pltpu.SMEM)
+    hbm = pl.BlockSpec(memory_space=pltpu.MemorySpace.HBM)
     dma = pltpu.SemaphoreType.DMA
-    return pl.pallas_call(
+    results = pl.pallas_call(
         functools.partial(fused_kernel, owners, rays, reps),
         out_shape=(
-            jax.ShapeDtypeStruct(targets.shape, F32),
+            jax.ShapeDtypeStruct((1, targets.shape[0]), F32),
             jax.ShapeDtypeStruct((bricks, share, hidden), F32),
             jax.ShapeDtypeStruct((bricks, share, hidden), F32),
             jax.ShapeDtypeStruct((bricks, out, share), F32),
         ),
-        in_specs=[smem, smem, vmem, vmem, vmem, vmem, vmem],
+        in_specs=[smem, smem, hbm, hbm, hbm, hbm, hbm],
         out_specs=(vmem, vmem, vmem, vmem),
         scratch_shapes=[
             pltpu.VMEM((owners, 32, pair), BF16),
@@ -564,11 +607,17 @@
             pltpu.VMEM((owners, 8, pair), F32),
             pltpu.VMEM((owners, 16, pair), BF16),
             pltpu.VMEM((groups, owners, 16, pair), BF16),
+            pltpu.VMEM(samples.shape, BF16),
+            pltpu.VMEM(frequencies.shape, F32),
+            pltpu.VMEM(w_first.shape, BF16),
+            pltpu.VMEM(w_second.shape, BF16),
+            pltpu.VMEM(w_out.shape, BF16),
             pltpu.VMEM((groups, features, wide), BF16),
             pltpu.VMEM((groups, hidden, wide), BF16),
             pltpu.VMEM((groups, hidden, wide), BF16),
             pltpu.VMEM((groups, hidden, wide), F32),
             pltpu.VMEM((groups, hidden, wide), F32),
+            dma((5,)),
             dma((owners,)),
             dma((owners,)),
             dma((groups,)),
@@ -579,9 +628,19 @@
             dma((groups, owners)),
         ],
         compiler_params=pltpu.CompilerParams(
-            collective_id=0, has_side_effects=True, vmem_limit_bytes=40 * 1024 * 1024
+            collective_id=0, has_side_effects=True,
+            vmem_limit_bytes=63 * 1024 * 1024,
         ),
-    )(brick_ids, targets, samples, frequencies, w_first, w_second, w_out)
+    )(brick_ids, targets.T, samples, frequencies, w_first, w_second, w_out)
+    predicted, grad_first, grad_second, grad_last = pl.pallas_call(
+        place_kernel,
+        out_shape=tuple(jax.ShapeDtypeStruct(r.shape, r.dtype) for r in results),
+        in_specs=[hbm] * 4,
+        out_specs=(hbm,) * 4,
+        scratch_shapes=[dma((4,))],
+        compiler_params=pltpu.CompilerParams(vmem_limit_bytes=63 * 1024 * 1024),
+    )(*results)
+    return predicted.T, grad_first, grad_second, grad_last
 
 
 def on_device(samples, frequencies, w_first, w_second, w_out, brick_ids, targets):

time: 29.7 us -> 27.5 us (0.926)
  local copies, waits for them, and re-layouts: 7.11 us -> 0 us
  Pallas kernels: 21.5 us -> 26.6 us
    unnamed x16 -> x0, local copies, waits for them, and re-layouts: 6.51 us -> none
    pallas_call x0 -> x1, Pallas kernels: none -> 5.37 us  [fused_plan(): pl.pallas_call(place_kernel, out_shape=tuple((jax.ShapeDtypeStruct(r.shap...]
    pallas_call x1 -> x0, local copies, waits for them, and re-layouts: 0.6 us -> none  [fused_plan(): pl.pallas_call(functools.partial(fused_kernel, owners, rays, reps), out_s...]
    pallas_call x1, Pallas kernels: 21.5 us -> 21.2 us  [fused_plan(): pl.pallas_call(functools.partial(fused_kernel, owners, rays, reps), out_s...]
where the time goes in v2:
time: 27.5 us; the launch traced here: 27.2 us
  Pallas kernels  26.6 us (97%)
  between operations  0.64 us (2%)
    pallas_call x1, Pallas kernels, fused_plan(): pl.pallas_call(functools.partial(fused_kernel, owners, rays, reps), out_s...  21.2 us
    pallas_call x1, Pallas kernels, fused_plan(): pl.pallas_call(place_kernel, out_shape=tuple((jax.ShapeDtypeStruct(r.shap...  5.37 us

profile of v2, /device:TPU:0, one launch (start us, length us, event | category | flops | bytes accessed | tf_op | source)
XLA Modules:
  0.0 27.2 jit_solution(14210299678282614076)
XLA Ops:
  0.6 21.2 %shard_map.102 = (f32[1,3]{1,0:T(1,128)}, f32[4,32,128]{2,1,0:T(8,128)}, f32[4,32,128]{2,1,0:T(8,128)}, f32[4,4,32]{2,1,0:T(4,128)}) custom-call(s32[1,4]{1,0:T(1,128)} %ids_ref.1, f32[1,3]{1,0:T(1,128)} %bitcast.2, bf16[1,4,16,64]{3,2,1,0:T(8,128)(2,1)} %samples_hbm.1, f32[16,64]{1,0:T(8,128)} %freq_hbm.1, bf16[4,128,128]{2,1,0:T(8,128)(2,1)} %w1_hbm.1, ...), custom_call_target="tpu_custom_call" | custom-call | tf_op jit(solution)/shard_map/pallas_call | solution.py:593
  21.8 5.4 %shard_map.103 = (f32[1,3]{1,0:T(1,128)}, f32[4,32,128]{2,1,0:T(8,128)}, f32[4,32,128]{2,1,0:T(8,128)}, f32[4,4,32]{2,1,0:T(4,128)}) custom-call(f32[1,3]{1,0:T(1,128)} %get-tuple-element.12.refs_0_, f32[4,32,128]{2,1,0:T(8,128)} %get-tuple-element.13.refs_1_, f32[4,32,128]{2,1,0:T(8,128)} %get-tuple-element.14.refs_2_, f32[4,4,32]{2,1,0:T(4,128)} %get-tuple-element.15.refs_3_), custom_call_target="tpu_custom_call" | custom-call | tf_op jit(solution)/shard_map/pallas_call | solution.py:635

commit v3 on v2

--- a/solution.py
+++ b/solution.py
@@ -214,10 +214,7 @@
     w1_hbm,
     w2_hbm,
     wo_hbm,
-    pred_ref,
-    gf_ref,
-    gs_ref,
-    go_ref,
+    packed_ref,
     sx,
     rx,
     sf,
@@ -494,7 +491,11 @@
         miss = loss_scale * (predicted - targets_ref[0, c])
         pull.append(miss * weights)
         lifted = lifted + miss * signal
-    pred_ref[...] = jnp.concatenate(predictions, axis=1)
+    packed_ref[0:8] = jnp.concatenate(
+        [jnp.zeros((8, 1), F32) + p for p in predictions]
+        + [jnp.zeros((8, hidden - len(predictions)), F32)],
+        axis=1,
+    )
     product = lifted * weights
     after = summed(product, lower) + offsets(product, True)
     density_grad = (
@@ -554,25 +555,17 @@
         gs = gs + nt(masked(h1_s[d, mine, :], mask), d2)
         go = go + nt(rows16, h2_s[d, mine, :])
         gf = gf + nt(masked(enc_s[d, mine, :], mask), d1)
-    for b in range(bricks):
-        gf_ref[b] = gf[b * share : (b + 1) * share]
-        gs_ref[b] = gs[b * share : (b + 1) * share]
-        go_ref[b] = go[b * channels_out : (b + 1) * channels_out]
+    at = 8
+    for block in (
+        jnp.concatenate([go, jnp.zeros((go.shape[0], hidden - share), F32)], axis=1),
+        gf,
+        gs,
+    ):
+        packed_ref[at : at + block.shape[0]] = block
+        at = at + block.shape[0]
 
     for copy in started:
         copy.wait_send()
-
-
-def place_kernel(*refs):
-    sources, targets, sem = refs[:4], refs[4:8], refs[8]
-    copies = [
-        pltpu.make_async_copy(source, target, sem.at[i])
-        for i, (source, target) in enumerate(zip(sources, targets))
-    ]
-    for copy in copies:
-        copy.start()
-    for copy in copies:
-        copy.wait()
 
 
 def fused_plan(samples, frequencies, w_first, w_second, w_out, brick_ids, targets):
@@ -590,16 +583,11 @@
     smem = pl.BlockSpec(memory_space=pltpu.SMEM)
     hbm = pl.BlockSpec(memory_space=pltpu.MemorySpace.HBM)
     dma = pltpu.SemaphoreType.DMA
-    results = pl.pallas_call(
+    packed = pl.pallas_call(
         functools.partial(fused_kernel, owners, rays, reps),
-        out_shape=(
-            jax.ShapeDtypeStruct((1, targets.shape[0]), F32),
-            jax.ShapeDtypeStruct((bricks, share, hidden), F32),
-            jax.ShapeDtypeStruct((bricks, share, hidden), F32),
-            jax.ShapeDtypeStruct((bricks, out, share), F32),
-        ),
+        out_shape=jax.ShapeDtypeStruct((8 + bricks * (out + 2 * share), hidden), F32),
         in_specs=[smem, smem, hbm, hbm, hbm, hbm, hbm],
-        out_specs=(vmem, vmem, vmem, vmem),
+        out_specs=vmem,
         scratch_shapes=[
             pltpu.VMEM((owners, 32, pair), BF16),
             pltpu.VMEM((groups, owners, 32, pair), BF16),
@@ -632,15 +620,14 @@
             vmem_limit_bytes=63 * 1024 * 1024,
         ),
     )(brick_ids, targets.T, samples, frequencies, w_first, w_second, w_out)
-    predicted, grad_first, grad_second, grad_last = pl.pallas_call(
-        place_kernel,
-        out_shape=tuple(jax.ShapeDtypeStruct(r.shape, r.dtype) for r in results),
-        in_specs=[hbm] * 4,
-        out_specs=(hbm,) * 4,
-        scratch_shapes=[dma((4,))],
-        compiler_params=pltpu.CompilerParams(vmem_limit_bytes=63 * 1024 * 1024),
-    )(*results)
-    return predicted.T, grad_first, grad_second, grad_last
+    signals = targets.shape[0]
+    last, first, second = 8, 8 + bricks * out, 8 + bricks * (out + share)
+    return (
+        packed[:1, :signals].T,
+        packed[first:second].reshape(bricks, share, hidden),
+        packed[second:].reshape(bricks, share, hidden),
+        packed[last:first, :share].reshape(bricks, out, share),
+    )
 
 
 def on_device(samples, frequencies, w_first, w_second, w_out, brick_ids, targets):

time: 27.5 us -> 26.2 us (0.953)
  Pallas kernels: 26.6 us -> 21.2 us
  local copies, waits for them, and re-layouts: 0 us -> 4 us
    pallas_call x1 -> x0, Pallas kernels: 5.37 us -> none  [fused_plan(): pl.pallas_call(place_kernel, out_shape=tuple((jax.ShapeDtypeStruct(r.shap...]
    slice x0 -> x2, local copies, waits for them, and re-layouts: none -> 2.82 us  [the longest x1 1.53 us: fused_plan(): packed[second:].reshape(bricks, share, hidden)]
    transpose x0 -> x1, local copies, waits for them, and re-layouts: none -> 1.18 us  [fused_plan(): packed[:1, :signals]]
where the time goes in v3:
time: 26.2 us; the launch traced here: 25.8 us
  Pallas kernels  21.2 us (81%)
  local copies, waits for them, and re-layouts  4 us (15%)
  between operations  0.64 us (2%)
    pallas_call x1, Pallas kernels, fused_plan(): pl.pallas_call(functools.partial(fused_kernel, owners, rays, reps), out_s...  21.2 us
    slice x1, local copies, waits for them, and re-layouts, fused_plan(): packed[second:].reshape(bricks, share, hidden)  1.53 us
    slice x1, local copies, waits for them, and re-layouts, fused_plan(): packed[last:first, :share].reshape(bricks, out, share)  1.29 us
    transpose x1, local copies, waits for them, and re-layouts, fused_plan(): packed[:1, :signals]  1.18 us

profile of v3, /device:TPU:0, one launch (start us, length us, event | category | flops | bytes accessed | tf_op | source)
XLA Modules:
  0.0 25.8 jit_solution(295179480837999928)
XLA Ops:
  0.6 21.2 %shard_map.102 = f32[280,128]{1,0:T(8,128)} custom-call(s32[1,4]{1,0:T(1,128)} %ids_ref.1, f32[1,3]{1,0:T(1,128)} %bitcast.9, bf16[1,4,16,64]{3,2,1,0:T(8,128)(2,1)} %samples_hbm.1, f32[16,64]{1,0:T(8,128)} %freq_hbm.1, bf16[4,128,128]{2,1,0:T(8,128)(2,1)} %w1_hbm.1, bf16[4,128,128]{2,1,0:T(8,128)(2,1)} %w2_hbm.1, bf16[4,4,128]{2,1,0:T(4,128)(2,1)} %wo_hbm.1), custom_call_target="tpu_custom_call" | custom-call | tf_op jit(solution)/shard_map/pallas_call | solution.py:586
  21.8 1.5 %fusion = (f32[128,128]{1,0:T(8,128)}, f32[128,128]{1,0:T(8,128)}) fusion(f32[280,128]{1,0:T(8,128)} %shard_map.102), kind=kLoop, calls=%fused_computation.1 | loop fusion | bytes 262144 | tf_op jit(solution)/shard_map/slice | solution.py:628
  23.4 1.3 %slice.15 = f32[16,32]{1,0:T(8,128)} slice(f32[280,128]{1,0:T(8,128)} %shard_map.102), slice={[8:24], [0:32]} | slice | bytes 4096 | tf_op jit(solution)/shard_map/slice | solution.py:629
  24.7 1.2 %slice_bitcast_fusion = f32[3,1]{0,1:T(1,128)} fusion(f32[280,128]{1,0:T(8,128)} %shard_map.102), kind=kLoop, calls=%fused_computation | loop fusion | bytes 24 | tf_op jit(solution)/shard_map/transpose | solution.py:626
